TPU v7x, 32 devices: a whole 2x2x4 slice. The times are simulated.
32 devices in a mesh: dp: 4 (over y, x), expert: 8 (over z, core).
Axes of the slice: x: 2, y: 2, z: 4, core: 2. Of those that a mesh axis runs over, the one named last changes fastest.
Arguments:
- tokens: bfloat16 [4096, 2560], P(('dp', 'expert')), may hold values from -6 to 6
- routes: int32 [4096, 2], P(('dp', 'expert')), may hold values from 0 to 7, all different within a row; in each aligned block of 128 rows (0 to 127, 128 to 255, ...) at most 36 rows name the same one
- route_gates: float32 [4096, 2], P(('dp', 'expert')), may hold values from 0.2 to 1
- w_gate: bfloat16 [8, 2560, 768], P('expert', 'dp'), may hold values from -0.125 to 0.125
- w_up: bfloat16 [8, 2560, 768], P('expert', 'dp'), may hold values from -0.125 to 0.125
- w_down: bfloat16 [8, 768, 2560], P('expert', None, 'dp'), may hold values from -0.21875 to 0.21875
- cotangent: bfloat16 [4096, 2560], P(('dp', 'expert')), may hold values from -6 to 6
Outputs:
- layer_out: bfloat16 [4096, 2560], P(('dp', 'expert'))
- token_grad: bfloat16 [4096, 2560], P(('dp', 'expert'))
- gate_grad: float32 [4096, 2], P(('dp', 'expert'))
Inputs may be any that keep to these rules, and one draw needn't show every extreme that they name: `routes`: among the 128 rows of one device, each expert is named at most 36 times, and in every draw some device names some expert exactly 36 times. The 2 experts of a token differ.
All inputs are finite; a program needn't handle non-finite values.
Results may differ from a plain program's by a relative error of at most 0.0067.
Values may be sent and summed in bfloat16 or wider, within the bound.
A program may use at most 128 MiB of HBM per device.

v0:
```python
import jax
import jax.numpy as jnp
from jax import lax
from jax.sharding import PartitionSpec as P

EXP_DEV = 1


def expert_forward(arriving, gate_full, up_full, down_full):
    gate_pre = jnp.einsum("snd,df->snf", arriving, gate_full, preferred_element_type=jnp.float32)
    up_pre = jnp.einsum("snd,df->snf", arriving, up_full, preferred_element_type=jnp.float32)
    hidden = (gate_pre * jax.nn.sigmoid(gate_pre) * up_pre).astype(jnp.bfloat16)
    expert_out = jnp.einsum(
        "snf,fd->snd", hidden, down_full, preferred_element_type=jnp.float32
    ).astype(jnp.bfloat16)
    return (expert_out, gate_pre, up_pre)


def expert_backward(arriving_grad, gate_pre, up_pre, gate_full, up_full, down_full):
    hidden_grad = jnp.einsum(
        "snd,fd->snf", arriving_grad, down_full, preferred_element_type=jnp.float32
    )
    logistic = jax.nn.sigmoid(gate_pre)
    pre_gate = (hidden_grad * up_pre * logistic * (1.0 + gate_pre * (1.0 - logistic))).astype(
        jnp.bfloat16
    )
    pre_up = (hidden_grad * gate_pre * logistic).astype(jnp.bfloat16)
    input_grad = jnp.einsum("snf,df->snd", pre_gate, gate_full, preferred_element_type=jnp.float32)
    input_grad = input_grad + jnp.einsum(
        "snf,df->snd", pre_up, up_full, preferred_element_type=jnp.float32
    )
    return input_grad.astype(jnp.bfloat16)


def local(tokens, routes, route_gates, w_gate, w_up, w_down, cotangent):
    groups = lax.axis_size("expert")
    tok_rows = tokens.shape[0]
    top_count = routes.shape[1]
    width = tokens.shape[1]
    capacity = 9 * tok_rows * top_count // (8 * groups * EXP_DEV)
    pair_expert = routes.reshape(-1)
    pair_token = jnp.arange(tok_rows * top_count, dtype=jnp.int32) // top_count
    onehot = (pair_expert[:, None] == jnp.arange(groups, dtype=jnp.int32)[None, :]).astype(
        jnp.int32
    )
    slot_rank = jnp.sum((jnp.cumsum(onehot, axis=0) - onehot) * onehot, axis=1)
    slot_place = pair_expert * capacity + slot_rank
    outbox = (
        jnp.zeros((groups * capacity, width), jnp.bfloat16).at[slot_place].set(tokens[pair_token])
    )
    outbox = outbox.reshape(groups, capacity, width)
    pair_gate = route_gates.reshape(-1)
    cot_pairs = cotangent[pair_token].astype(jnp.float32)
    row_grad = (pair_gate[:, None] * cot_pairs).astype(jnp.bfloat16)
    gradbox = jnp.zeros((groups * capacity, width), jnp.bfloat16).at[slot_place].set(row_grad)
    gradbox = gradbox.reshape(groups, capacity, width)
    gate_full, up_full, down_full = (
        lax.all_gather(w_gate[0], "dp", axis=0, tiled=True),
        lax.all_gather(w_up[0], "dp", axis=0, tiled=True),
        lax.all_gather(w_down[0], "dp", axis=1, tiled=True),
    )
    expert_out, gate_pre, up_pre = expert_forward(
        lax.all_to_all(outbox, "expert", split_axis=0, concat_axis=0, tiled=True),
        gate_full,
        up_full,
        down_full,
    )
    returned = lax.all_to_all(expert_out, "expert", split_axis=0, concat_axis=0, tiled=True)
    returned, gate_pre, up_pre = (returned, gate_pre, up_pre)
    arriving_grad = lax.all_to_all(gradbox, "expert", split_axis=0, concat_axis=0, tiled=True)
    input_grad = expert_backward(arriving_grad, gate_pre, up_pre, gate_full, up_full, down_full)
    back_grad = lax.all_to_all(input_grad, "expert", split_axis=0, concat_axis=0, tiled=True)
    pair_out = returned.reshape(groups * capacity, width)[slot_place].astype(jnp.float32)
    layer_out = jnp.sum(
        (pair_gate[:, None] * pair_out).reshape(tok_rows, top_count, width), axis=1
    ).astype(jnp.bfloat16)
    gate_grad = jnp.sum(cot_pairs * pair_out, axis=1).reshape(tok_rows, top_count)
    pair_grad = back_grad.reshape(groups * capacity, width)[slot_place].astype(jnp.float32)
    token_grad = jnp.sum(pair_grad.reshape(tok_rows, top_count, width), axis=1).astype(jnp.bfloat16)
    return (layer_out, token_grad, gate_grad)


def solution(mesh):
    in_specs = (
        P(("dp", "expert"), None),
        P(("dp", "expert"), None),
        P(("dp", "expert"), None),
        P("expert", "dp", None),
        P("expert", "dp", None),
        P("expert", None, "dp"),
        P(("dp", "expert"), None),
    )
    out_specs = (P(("dp", "expert"), None), P(("dp", "expert"), None), P(("dp", "expert"), None))
    return jax.shard_map(local, mesh=mesh, in_specs=in_specs, out_specs=out_specs, check_vma=False)
```

profile of v0, /device:TPU:0, one launch (start us, length us, event | category | flops | bytes accessed | tf_op | source)
XLA Modules:
  0.0 285.9 jit_solution(3171517548182173325)
XLA Ops:
  7.2 0.0 copy-start
  7.2 0.0 copy-start.4
  7.2 0.0 all-gather.7.cloned.1.call-start
  7.2 0.7 all-gather.7.cloned.1.call-update
  7.9 0.0 all-gather.9.cloned.1.call-start
  8.0 0.7 all-gather.9.cloned.1.call-update
  8.7 0.0 all-gather.11.cloned.1.call-start
  8.7 0.7 all-gather.11.cloned.1.call-update
  9.4 0.0 copy-done.4
  9.4 0.1 copy.13
  9.5 0.1 eq.29
  9.7 0.1 eq.25
  9.8 0.1 copy.12
  9.9 0.1 mul.68
  10.1 0.6 reduce-window.6
  10.7 0.2 slice_reduce_fusion
  11.0 0.1 fusion.24
  11.1 0.0 copy-done
  11.1 6.9 %scatter_custom_fusion = bf16[288,2560]{1,0:T(8,128)(2,1)S(1)} fusion(s32[256]{0:T(256)S(1)} %bitcast.34, bf16[128,2560]{1,0:T(8,128)(2,1)S(1)} %copy-done, s32[1024]{0:T(1024)S(1)} %pad_clamp_fusion.1, bf16[]{:T(256)} %constant.26.clone.1), kind=kCustom, calls=%fused_computation.25 | custom fusion | bytes 1474562 | tf_op jit(solution)/shard_map/scatter | solution.py:49
  18.0 1.4 reshape.123
  19.3 0.0 copy-start.5
  19.3 0.0 copy-start.1
  19.3 6.5 %all-to-all-start = ((bf16[8,36,2560]{2,1,0:T(8,128)(2,1)}), bf16[8,36,2560]{2,1,0:T(8,128)(2,1)}, u32[]{:S(2)}, u32[]{:S(2)}) async-start(bf16[8,36,2560]{2,1,0:T(8,128)(2,1)} %reshape.123), calls=%async_computation | async-start | bytes 3276800 | tf_op jit(solution)/shard_map/all_to_all | solution.py:63
  25.8 0.0 copy-done.5
  25.8 0.1 copy.11
  25.9 0.1 mul.73
  26.0 0.0 copy-done.1
  26.1 1.4 gather_fusion.1
  27.5 3.1 %scatter_custom_fusion.1 = bf16[288,2560]{1,0:T(8,128)(2,1)S(1)} fusion(s32[256]{0:T(256)S(1)} %bitcast.35, bf16[256,2560]{1,0:T(8,128)(2,1)S(1)} %gather_fusion.1, f32[256]{0:T(256)S(1)} %mul.73, bf16[]{:T(256)} %constant.26.clone.1), kind=kCustom, calls=%fused_computation.24 | custom fusion | flops 1966080 | bytes 2786306 | tf_op jit(solution)/shard_map/scatter | solution.py:55
  30.6 1.4 reshape.125
  32.1 33.1 %all-to-all-done = bf16[8,36,2560]{2,1,0:T(8,128)(2,1)} async-done(((bf16[8,36,2560]{2,1,0:T(8,128)(2,1)}), bf16[8,36,2560]{2,1,0:T(8,128)(2,1)}, u32[]{:S(2)}, u32[]{:S(2)}) %all-to-all-start) | async-done | bytes 1474592 | tf_op jit(solution)/shard_map/all_to_all | solution.py:63
  65.1 4.3 %all-to-all-start.2 = ((bf16[8,36,2560]{2,1,0:T(8,128)(2,1)}), bf16[8,36,2560]{2,1,0:T(8,128)(2,1)}, u32[]{:S(2)}, u32[]{:S(2)}) async-start(bf16[8,36,2560]{2,1,0:T(8,128)(2,1)} %reshape.125), calls=%async_computation.2 | async-start | bytes 3276800 | tf_op jit(solution)/shard_map/all_to_all | solution.py:70
  69.4 0.0 all-gather.7.cloned.1.call-done
  69.5 4.3 %fusion.9 = f32[8,36,768]{2,1,0:T(8,128)S(1)} fusion(bf16[8,36,2560]{2,1,0:T(8,128)(2,1)} %all-to-all-done, bf16[1,2560,768]{2,1,0:T(8,128)(2,1)} %all-gather.7.cloned.1.call-done), kind=kOutput, calls=%fused_computation.17 | convolution fusion | flops 1132462080 | bytes 6291456 | tf_op jit(solution)/shard_map/snd,df->snf/dot_general | solution.py:10
  73.8 41.8 %all-gather.9.cloned.1.call-done = bf16[1,2560,768]{2,1,0:T(8,128)(2,1)} async-done(((bf16[1,640,768]{2,1,0:T(8,128)(2,1)}), bf16[1,2560,768]{2,1,0:T(8,128)(2,1)}) %all-gather.9.cloned.1.call-update) | async-done | bytes 3932176 | tf_op jit(solution)/shard_map/all_gather | solution.py:59
  115.5 5.0 %fusion.5 = f32[8,36,768]{2,1,0:T(8,128)} fusion(bf16[8,36,2560]{2,1,0:T(8,128)(2,1)} %all-to-all-done, bf16[1,2560,768]{2,1,0:T(8,128)(2,1)} %all-gather.9.cloned.1.call-done), kind=kOutput, calls=%fused_computation.13 | convolution fusion | flops 1132462080 | bytes 6291456 | tf_op jit(solution)/shard_map/snd,df->snf/dot_general | solution.py:11
  120.6 47.4 %all-gather.11.cloned.1.call-done = bf16[1,768,2560]{2,1,0:T(8,128)(2,1)} async-done(((bf16[1,768,640]{2,1,0:T(8,128)(2,1)}), bf16[1,768,2560]{2,1,0:T(8,128)(2,1)}) %all-gather.11.cloned.1.call-update) | async-done | bytes 3932176 | tf_op jit(solution)/shard_map/all_gather | solution.py:60
  167.9 5.1 %convolution_convert_fusion = bf16[8,36,2560]{2,1,0:T(8,128)(2,1)} fusion(bf16[1,768,2560]{2,1,0:T(8,128)(2,1)} %all-gather.11.cloned.1.call-done, f32[8,36,768]{2,1,0:T(8,128)} %fusion.5, f32[8,36,768]{2,1,0:T(8,128)S(1)} %fusion.9), kind=kOutput, calls=%fused_computation.8 | convolution fusion | flops 1134526464 | bytes 7176192 | tf_op jit(solution)/shard_map/snf,fd->snd/dot_general | solution.py:13
  173.0 0.0 all-to-all-done.2
  173.0 4.6 %all-to-all-start.1 = ((bf16[8,36,2560]{2,1,0:T(8,128)(2,1)}), bf16[8,36,2560]{2,1,0:T(8,128)(2,1)}, u32[]{:S(2)}, u32[]{:S(2)}) async-start(bf16[8,36,2560]{2,1,0:T(8,128)(2,1)} %convolution_convert_fusion), calls=%async_computation.1 | async-start | bytes 3276800 | tf_op jit(solution)/shard_map/all_to_all | solution.py:68
  177.7 0.0 copy-start.8
  177.7 4.2 %fusion.1 = f32[8,36,768]{2,1,0:T(8,128)S(1)} fusion(bf16[8,36,2560]{2,1,0:T(8,128)(2,1)} %all-to-all-done.2, bf16[1,768,2560]{2,1,0:T(8,128)(2,1)} %all-gather.11.cloned.1.call-done), kind=kOutput, calls=%fused_computation.9 | convolution fusion | flops 1132462080 | bytes 6291456 | tf_op jit(solution)/shard_map/snd,fd->snf/dot_general | solution.py:20
  181.9 0.0 copy-done.6
  181.9 0.0 copy-done.8
  181.9 0.0 copy-start.7
  181.9 1.7 fusion.7
  183.6 0.4 copy-done.7
  184.0 2.7 fusion
  186.8 30.2 %all-to-all-done.1 = bf16[8,36,2560]{2,1,0:T(8,128)(2,1)} async-done(((bf16[8,36,2560]{2,1,0:T(8,128)(2,1)}), bf16[8,36,2560]{2,1,0:T(8,128)(2,1)}, u32[]{:S(2)}, u32[]{:S(2)}) %all-to-all-start.1) | async-done | bytes 1474592 | tf_op jit(solution)/shard_map/all_to_all | solution.py:68
  217.0 4.3 %all-to-all-start.3 = ((bf16[8,36,2560]{2,1,0:T(8,128)(2,1)}), bf16[8,36,2560]{2,1,0:T(8,128)(2,1)}, u32[]{:S(2)}, u32[]{:S(2)}) async-start(bf16[8,36,2560]{2,1,0:T(8,128)(2,1)} %fusion), calls=%async_computation.3 | async-start | bytes 3276800 | tf_op jit(solution)/shard_map/all_to_all | solution.py:72
  221.3 1.6 reshape.124
  222.9 2.5 gather_fusion
  225.4 4.2 %reshape.128 = f32[128,2,2560]{2,1,0:T(2,128)} reshape(bf16[256,2560]{1,0:T(8,128)(2,1)} %gather_fusion) | data formatting | bytes 3932160 | tf_op jit(solution)/shard_map/convert_element_type | solution.py:73
  229.6 0.0 copy-done.2
  229.6 0.4 fusion.12
  230.1 30.5 %all-to-all-done.3 = bf16[8,36,2560]{2,1,0:T(8,128)(2,1)} async-done(((bf16[8,36,2560]{2,1,0:T(8,128)(2,1)}), bf16[8,36,2560]{2,1,0:T(8,128)(2,1)}, u32[]{:S(2)}, u32[]{:S(2)}) %all-to-all-start.3) | async-done | bytes 1474592 | tf_op jit(solution)/shard_map/all_to_all | solution.py:72
  260.5 1.5 reshape.126
  262.1 2.5 gather_fusion.2
  264.6 4.1 %gather.18 = bf16[128,2,2560]{2,1,0:T(2,128)(2,1)} reshape(bf16[256,2560]{1,0:T(8,128)(2,1)} %gather_fusion.2) | data formatting | bytes 2621440 | tf_op jit(solution)/shard_map/gather | solution.py:78
  268.7 5.3 %reduce_sum.44 = bf16[128,2560]{1,0:T(8,128)(2,1)} reduce(bf16[128,2,2560]{2,1,0:T(2,128)(2,1)} %gather.18, bf16[]{:T(256)} %constant.26.clone.1), dimensions={1}, to_apply=%region_6.7 | reduce | flops 327680 | bytes 1966082 | tf_op jit(solution)/shard_map/reduce_sum | solution.py:79
  274.0 0.1 reshape.127
  274.2 0.6 copy.16
  274.8 0.0 copy-done.3
  274.8 4.5 %multiply_reduce_fusion = bf16[128,2560]{1,0:T(8,128)(2,1)} fusion(f32[128,2,2560]{2,1,0:T(2,128)S(1)} %copy-done.3, f32[128,2]{1,0:T(8,128)S(1)} %copy.11), kind=kLoop, calls=%fused_computation.23 | loop fusion | flops 983040 | bytes 3277824 | tf_op jit(solution)/shard_map/reduce_sum | solution.py:74
  (11 shorter events, 0.1 us)
Async XLA Ops:
  7.2 3.9 %copy-start = (bf16[128,2560]{1,0:T(8,128)(2,1)S(1)}, bf16[128,2560]{1,0:T(8,128)(2,1)}, u32[]{:S(2)}) copy-start(bf16[128,2560]{1,0:T(8,128)(2,1)} %param.7) | copy-start | bytes 1966084
  7.2 2.2 copy-start.4
  7.2 62.3 %all-gather.7.cloned.1.call-start = ((), (), s32[]{:S(2)}) async-start(), calls=%async_computation.4 | async-start | bytes 4915200 | tf_op jit(solution)/shard_map/all_gather | solution.py:58
  7.9 107.6 %all-gather.9.cloned.1.call-start = ((), (), s32[]{:S(2)}) async-start(), calls=%async_computation.5 | async-start | bytes 4915200 | tf_op jit(solution)/shard_map/all_gather | solution.py:59
  8.7 159.3 %all-gather.11.cloned.1.call-start = ((), (), s32[]{:S(2)}) async-start(), calls=%async_computation.6 | async-start | bytes 4915200 | tf_op jit(solution)/shard_map/all_gather | solution.py:60
  19.3 6.5 %copy-start.5 = (f32[128,2]{0,1:T(2,128)S(1)}, f32[128,2]{0,1:T(2,128)}, u32[]{:S(2)}) copy-start(f32[128,2]{0,1:T(2,128)} %param.9) | copy-start | bytes 3076
  19.3 6.7 %copy-start.1 = (bf16[128,2560]{1,0:T(8,128)(2,1)S(1)}, bf16[128,2560]{1,0:T(8,128)(2,1)}, u32[]{:S(2)}) copy-start(bf16[128,2560]{1,0:T(8,128)(2,1)} %param.13) | copy-start | bytes 1966084
  19.3 45.8 %all-to-all-start = ((bf16[8,36,2560]{2,1,0:T(8,128)(2,1)}), bf16[8,36,2560]{2,1,0:T(8,128)(2,1)}, u32[]{:S(2)}, u32[]{:S(2)}) async-start(bf16[8,36,2560]{2,1,0:T(8,128)(2,1)} %reshape.123), calls=%async_computation | async-start | bytes 3276800 | tf_op jit(solution)/shard_map/all_to_all | solution.py:63
  65.1 107.9 %all-to-all-start.2 = ((bf16[8,36,2560]{2,1,0:T(8,128)(2,1)}), bf16[8,36,2560]{2,1,0:T(8,128)(2,1)}, u32[]{:S(2)}, u32[]{:S(2)}) async-start(bf16[8,36,2560]{2,1,0:T(8,128)(2,1)} %reshape.125), calls=%async_computation.2 | async-start | bytes 3276800 | tf_op jit(solution)/shard_map/all_to_all | solution.py:70
  173.0 43.9 %all-to-all-start.1 = ((bf16[8,36,2560]{2,1,0:T(8,128)(2,1)}), bf16[8,36,2560]{2,1,0:T(8,128)(2,1)}, u32[]{:S(2)}, u32[]{:S(2)}) async-start(bf16[8,36,2560]{2,1,0:T(8,128)(2,1)} %convolution_convert_fusion), calls=%async_computation.1 | async-start | bytes 3276800 | tf_op jit(solution)/shard_map/all_to_all | solution.py:68
  177.7 4.3 %copy-start.6 = (bf16[1,2560,768]{2,1,0:T(8,128)(2,1)S(1)}, bf16[1,2560,768]{2,1,0:T(8,128)(2,1)}, u32[]{:S(2)}) copy-start(bf16[1,2560,768]{2,1,0:T(8,128)(2,1)} %all-gather.7.cloned.1.call-done) | copy-start | bytes 11796484
  177.7 4.3 %copy-start.8 = (f32[8,36,768]{2,1,0:T(8,128)S(1)}, f32[8,36,768]{2,1,0:T(8,128)}, u32[]{:S(2)}) copy-start(f32[8,36,768]{2,1,0:T(8,128)} %fusion.5) | copy-start | bytes 2654212
  181.9 2.1 copy-start.7
  217.0 43.5 %all-to-all-start.3 = ((bf16[8,36,2560]{2,1,0:T(8,128)(2,1)}), bf16[8,36,2560]{2,1,0:T(8,128)(2,1)}, u32[]{:S(2)}, u32[]{:S(2)}) async-start(bf16[8,36,2560]{2,1,0:T(8,128)(2,1)} %fusion), calls=%async_computation.3 | async-start | bytes 3276800 | tf_op jit(solution)/shard_map/all_to_all | solution.py:72
  225.4 4.2 %copy-start.2 = (bf16[256,2560]{1,0:T(8,128)(2,1)S(1)}, bf16[256,2560]{1,0:T(8,128)(2,1)}, u32[]{:S(2)}) copy-start(bf16[256,2560]{1,0:T(8,128)(2,1)} %gather_fusion) | copy-start | bytes 3932164
  264.6 10.2 %copy-start.3 = (f32[128,2,2560]{2,1,0:T(2,128)S(1)}, f32[128,2,2560]{2,1,0:T(2,128)}, u32[]{:S(2)}) copy-start(f32[128,2,2560]{2,1,0:T(2,128)} %reshape.128) | copy-start | bytes 7864324
Sparse Core Ops, SparseCore 0:
  9.9 53.2 all-gather.6
  65.0 50.5 all-gather.8
  117.4 50.5 all-gather.10
where the time goes:
time: 286 us
  waiting for transfers between devices  185 us (65%)
  local copies, waits for them, and re-layouts  29.9 us (10%)
  matrix products  23.1 us (8%)
  starting transfers between devices  19.8 us (7%)
  other arithmetic  14.1 us (5%)
  between operations  14 us (5%)
    all_gather x1, waiting for transfers between devices, local(): lax.all_gather(w_down[0], 'dp', axis=1, tiled=True)  47.4 us
    all_gather x1, waiting for transfers between devices, local(): lax.all_gather(w_up[0], 'dp', axis=0, tiled=True)  41.8 us
    all_to_all x1, waiting for transfers between devices, local(): lax.all_to_all(outbox, 'expert', split_axis=0, concat_axis=0, tiled=True)  33.1 us
    all_to_all x1, waiting for transfers between devices, local(): lax.all_to_all(input_grad, 'expert', split_axis=0, concat_axis=0, tiled=T...  30.5 us
    all_to_all x1, waiting for transfers between devices, local(): lax.all_to_all(expert_out, 'expert', split_axis=0, concat_axis=0, tiled=T...  30.2 us
    scatter x1, local copies, waits for them, and re-layouts, local(): jnp.zeros((groups * capacity, width), jnp.bfloat16).at[slot_place]  6.87 us
    gather x2, local copies, waits for them, and re-layouts, local(): back_grad.reshape(groups * capacity, width)[slot_place].astype(jnp.float32)  6.62 us
    all_to_all x1, starting transfers between devices, local(): lax.all_to_all(outbox, 'expert', split_axis=0, concat_axis=0, tiled=True)  6.46 us
  transfers between devices with their start and end apart: 7, of which 5 were waited for; matrix products, arithmetic and copies ran while one was open for 17% of the time, Pallas kernels for 0%

commit v1 on v0

--- a/solution.py
+++ b/solution.py
@@ -1,9 +1,28 @@
+import functools
 import jax
 import jax.numpy as jnp
 from jax import lax
 from jax.sharding import PartitionSpec as P
 
 EXP_DEV = 1
+
+
+def plan_the_point(piece_in, dim_at):
+    outcome_arr = lax.axis_size("dp")
+    built, v_now = (outcome_arr, lax.axis_index("dp"))
+    inter, block_last = (piece_in, 1)
+    while block_last < built:
+        view_out = lax.ppermute(
+            inter, "dp", [(dev_j, dev_j ^ block_last) for dev_j in range(built)]
+        )
+        w_next = jnp.concatenate([inter, view_out], dim_at)
+        all_rows = jnp.concatenate([view_out, inter], dim_at)
+        inter = jnp.where(v_now & block_last == 0, w_next, all_rows)
+        block_last = 2 * block_last
+    return inter
+
+
+begin_the_roads = functools.partial(plan_the_point, dim_at=1)
 
 
 def expert_forward(arriving, gate_full, up_full, down_full):
@@ -57,7 +76,7 @@
     gate_full, up_full, down_full = (
         lax.all_gather(w_gate[0], "dp", axis=0, tiled=True),
         lax.all_gather(w_up[0], "dp", axis=0, tiled=True),
-        lax.all_gather(w_down[0], "dp", axis=1, tiled=True),
+        begin_the_roads(w_down[0]),
     )
     expert_out, gate_pre, up_pre = expert_forward(
         lax.all_to_all(outbox, "expert", split_axis=0, concat_axis=0, tiled=True),

time: 286 us -> 268 us (0.937)
  waiting for transfers between devices: 185 us -> 157 us
  starting transfers between devices: 19.8 us -> 23.1 us
  other arithmetic: 14.1 us -> 17.3 us
    all_gather x1 -> x0, waiting for transfers between devices: 47.4 us -> none  [local(): lax.all_gather(w_down[0], 'dp', axis=1, tiled=True)]
    ppermute x0 -> x2, waiting for transfers between devices: none -> 36.3 us  [plan_the_point(): lax.ppermute(inter, 'dp', [(dev_j, dev_j ^ block_last) for dev_j in range...]
    all_to_all x1, waiting for transfers between devices: 33.1 us -> 0.01 us  [local(): lax.all_to_all(outbox, 'expert', split_axis=0, concat_axis=0, tiled=True)]
    all_gather x1, waiting for transfers between devices: 41.8 us -> 60.2 us  [local(): lax.all_gather(w_up[0], 'dp', axis=0, tiled=True)]
    select_n x0 -> x1, other arithmetic: none -> 3.39 us  [plan_the_point(): inter = jnp.where(v_now & block_last == 0, w_next, all_rows)]
    ppermute x0 -> x2, starting transfers between devices: none -> 3.03 us  [plan_the_point(): lax.ppermute(inter, 'dp', [(dev_j, dev_j ^ block_last) for dev_j in range...]
  transfers between devices with their start and end apart: 7 -> 8, of which waited for: 5 -> 4; matrix products, arithmetic and copies ran while one was open for 17% -> 20% of each run, Pallas kernels for 0% -> 0%
where the time goes in v1:
time: 268 us; the launch traced here: 267 us
  waiting for transfers between devices  157 us (59%)
  local copies, waits for them, and re-layouts  30.7 us (11%)
  matrix products  24.7 us (9%)
  starting transfers between devices  23.1 us (9%)
  other arithmetic  17.3 us (6%)
  between operations  14.3 us (5%)
    all_gather x1, waiting for transfers between devices, local(): lax.all_gather(w_up[0], 'dp', axis=0, tiled=True)  60.2 us
    ppermute x2, waiting for transfers between devices, plan_the_point(): lax.ppermute(inter, 'dp', [(dev_j, dev_j ^ block_last) for dev_j in range...  36.3 us
    all_to_all x1, waiting for transfers between devices, local(): lax.all_to_all(input_grad, 'expert', split_axis=0, concat_axis=0, tiled=T...  30.5 us
    all_to_all x1, waiting for transfers between devices, local(): lax.all_to_all(expert_out, 'expert', split_axis=0, concat_axis=0, tiled=T...  28.5 us
    scatter x1, local copies, waits for them, and re-layouts, local(): jnp.zeros((groups * capacity, width), jnp.bfloat16).at[slot_place]  6.87 us
    gather x2, local copies, waits for them, and re-layouts, local(): back_grad.reshape(groups * capacity, width)[slot_place].astype(jnp.float32)  6.62 us
    all_to_all x1, starting transfers between devices, local(): lax.all_to_all(outbox, 'expert', split_axis=0, concat_axis=0, tiled=True)  6.48 us
    dot_general x1, matrix products, expert_forward(): jnp.einsum('snf,fd->snd', hidden, down_full, preferred_element_type=jnp.f...  6.27 us
  transfers between devices with their start and end apart: 8, of which 4 were waited for; matrix products, arithmetic and copies ran while one was open for 20% of the time, Pallas kernels for 0%

profile of v1, /device:TPU:0, one launch (start us, length us, event | category | flops | bytes accessed | tf_op | source)
XLA Modules:
  0.0 267.0 jit_solution(14918022140095998716)
XLA Ops:
  7.2 0.0 copy-start
  7.2 0.0 copy-start.5
  7.2 0.0 all-gather.5.cloned.1.call-start
  7.2 0.7 all-gather.5.cloned.1.call-update
  7.9 0.0 all-gather.7.cloned.1.call-start
  8.0 0.7 all-gather.7.cloned.1.call-update
  8.7 0.0 copy-done.5
  8.7 0.1 copy.13
  8.8 0.1 eq.35
  8.9 0.1 eq.31
  9.1 0.1 copy.12
  9.2 0.1 mul.68
  9.4 0.6 reduce-window.6
  9.9 0.2 slice_reduce_fusion
  10.2 0.1 fusion.25
  10.3 0.0 copy-done
  10.3 6.9 %scatter_custom_fusion = bf16[288,2560]{1,0:T(8,128)(2,1)S(1)} fusion(s32[256]{0:T(256)S(1)} %bitcast.35, bf16[128,2560]{1,0:T(8,128)(2,1)S(1)} %copy-done, s32[1024]{0:T(1024)S(1)} %pad_clamp_fusion.1, bf16[]{:T(256)} %constant.31.clone.1), kind=kCustom, calls=%fused_computation.26 | custom fusion | bytes 1474562 | tf_op jit(solution)/shard_map/scatter | solution.py:68
  17.2 1.3 reshape.123
  18.5 6.5 %all-to-all-start = ((bf16[8,36,2560]{2,1,0:T(8,128)(2,1)}), bf16[8,36,2560]{2,1,0:T(8,128)(2,1)}, u32[]{:S(2)}, u32[]{:S(2)}) async-start(bf16[8,36,2560]{2,1,0:T(8,128)(2,1)} %reshape.123), calls=%async_computation | async-start | bytes 3276800 | tf_op jit(solution)/shard_map/all_to_all | solution.py:82
  25.0 0.0 copy-done.4
  25.0 1.6 collective-permute-start
  26.6 36.3 %collective-permute-done = bf16[768,640]{1,0:T(8,128)(2,1)} collective-permute-done((bf16[768,640]{1,0:T(8,128)(2,1)S(1)}, bf16[768,640]{1,0:T(8,128)(2,1)}, u32[]{:S(2)}, u32[]{:S(2)}) %collective-permute-start) | collective-permute-done | bytes 983072 | tf_op jit(solution)/shard_map/ppermute | solution.py:15
  62.9 3.4 %maximum_select_fusion.1 = bf16[768,1280]{1,0:T(8,128)(2,1)} fusion(bf16[768,640]{1,0:T(8,128)(2,1)} %collective-permute-done, bf16[768,640]{1,0:T(8,128)(2,1)S(1)} %bitcast.34, pred[]{:T(512)S(6)} %eq.40), kind=kLoop, calls=%fused_computation.24 | loop fusion | flops 8847360 | bytes 3932161 | tf_op jit(solution)/shard_map/jit(_where)/select_n | solution.py:20
  66.3 1.5 collective-permute-start.1
  67.8 0.0 copy-done.6
  67.8 0.1 copy.11
  67.9 0.1 mul.73
  68.1 1.4 gather_fusion.1
  69.5 2.9 %scatter_custom_fusion.1 = bf16[288,2560]{1,0:T(8,128)(2,1)S(1)} fusion(s32[256]{0:T(256)S(1)} %bitcast.36, bf16[256,2560]{1,0:T(8,128)(2,1)S(1)} %gather_fusion.1, f32[256]{0:T(256)S(1)} %mul.73, bf16[]{:T(256)} %constant.31.clone.1), kind=kCustom, calls=%fused_computation.25 | custom fusion | flops 1966080 | bytes 2786306 | tf_op jit(solution)/shard_map/scatter | solution.py:74
  72.5 1.4 reshape.125
  73.8 0.0 all-to-all-done
  73.8 4.7 %all-to-all-start.2 = ((bf16[8,36,2560]{2,1,0:T(8,128)(2,1)}), bf16[8,36,2560]{2,1,0:T(8,128)(2,1)}, u32[]{:S(2)}, u32[]{:S(2)}) async-start(bf16[8,36,2560]{2,1,0:T(8,128)(2,1)} %reshape.125), calls=%async_computation.2 | async-start | bytes 3276800 | tf_op jit(solution)/shard_map/all_to_all | solution.py:89
  78.5 0.0 all-gather.5.cloned.1.call-done
  78.6 4.1 %fusion.7 = f32[8,36,768]{2,1,0:T(8,128)S(1)} fusion(bf16[8,36,2560]{2,1,0:T(8,128)(2,1)} %all-to-all-done, bf16[1,2560,768]{2,1,0:T(8,128)(2,1)} %all-gather.5.cloned.1.call-done), kind=kOutput, calls=%fused_computation.16 | convolution fusion | flops 1132462080 | bytes 6291456 | tf_op jit(solution)/shard_map/snd,df->snf/dot_general | solution.py:29
  82.6 60.2 %all-gather.7.cloned.1.call-done = bf16[1,2560,768]{2,1,0:T(8,128)(2,1)} async-done(((bf16[1,640,768]{2,1,0:T(8,128)(2,1)}), bf16[1,2560,768]{2,1,0:T(8,128)(2,1)}) %all-gather.7.cloned.1.call-update) | async-done | bytes 3932176 | tf_op jit(solution)/shard_map/all_gather | solution.py:78
  142.8 4.1 %fusion.3 = f32[8,36,768]{2,1,0:T(8,128)S(1)} fusion(bf16[8,36,2560]{2,1,0:T(8,128)(2,1)} %all-to-all-done, bf16[1,2560,768]{2,1,0:T(8,128)(2,1)} %all-gather.7.cloned.1.call-done), kind=kOutput, calls=%fused_computation.12 | convolution fusion | flops 1132462080 | bytes 6291456 | tf_op jit(solution)/shard_map/snd,df->snf/dot_general | solution.py:30
  146.9 0.0 collective-permute-done.1
  146.9 0.9 copy-done.9
  147.8 6.3 %convolution_convert_fusion = bf16[8,36,2560]{2,1,0:T(8,128)(2,1)} fusion(bf16[768,1280]{1,0:T(8,128)(2,1)} %collective-permute-done.1, bf16[768,1280]{1,0:T(8,128)(2,1)} %maximum_select_fusion.1, pred[]{:T(512)S(6)} %eq.39, f32[8,36,768]{2,1,0:T(8,128)S(1)} %fusion.3, f32[8,36,768]{2,1,0:T(8,128)S(1)} %fusion.7), kind=kOutput, calls=%fused_computation.8 | convolution fusion | flops 1152221184 | bytes 7176193 | tf_op jit(solution)/shard_map/snf,fd->snd/dot_general | solution.py:32
  154.1 0.0 all-to-all-done.2
  154.1 4.5 %all-to-all-start.1 = ((bf16[8,36,2560]{2,1,0:T(8,128)(2,1)}), bf16[8,36,2560]{2,1,0:T(8,128)(2,1)}, u32[]{:S(2)}, u32[]{:S(2)}) async-start(bf16[8,36,2560]{2,1,0:T(8,128)(2,1)} %convolution_convert_fusion), calls=%async_computation.1 | async-start | bytes 3276800 | tf_op jit(solution)/shard_map/all_to_all | solution.py:87
  158.6 0.0 copy-start.7
  158.6 0.0 copy-start.10
  158.6 5.8 %fusion.11 = f32[8,36,768]{2,1,0:T(8,128)S(1)} fusion(bf16[8,36,2560]{2,1,0:T(8,128)(2,1)} %all-to-all-done.2, bf16[768,1280]{1,0:T(8,128)(2,1)} %collective-permute-done.1, bf16[768,1280]{1,0:T(8,128)(2,1)} %maximum_select_fusion.1, pred[]{:T(512)S(6)} %eq.39), kind=kOutput, calls=%fused_computation.23 | convolution fusion | flops 1150156800 | bytes 6291457 | tf_op jit(solution)/shard_map/snd,fd->snf/dot_general | solution.py:39
  164.5 0.0 copy-done.7
  164.5 0.0 copy-done.10
  164.5 0.0 copy-start.8
  164.5 1.7 fusion.5
  166.2 0.4 copy-done.8
  166.6 2.7 %fusion = bf16[8,36,2560]{2,1,0:T(8,128)(2,1)} fusion(f32[8,36,2560]{2,1,0:T(8,128)S(1)} %fusion.5, bf16[1,2560,768]{2,1,0:T(8,128)(2,1)S(1)} %copy-done.8, f32[8,36,768]{2,1,0:T(8,128)S(1)} %fusion.11, f32[8,36,768]{2,1,0:T(8,128)S(1)} %fusion.7), kind=kOutput, calls=%fused_computation.7 | convolution fusion | flops 1135263744 | bytes 10125312 | tf_op jit(solution)/shard_map/snf,df->snd/dot_general | solution.py:48
  169.4 28.5 %all-to-all-done.1 = bf16[8,36,2560]{2,1,0:T(8,128)(2,1)} async-done(((bf16[8,36,2560]{2,1,0:T(8,128)(2,1)}), bf16[8,36,2560]{2,1,0:T(8,128)(2,1)}, u32[]{:S(2)}, u32[]{:S(2)}) %all-to-all-start.1) | async-done | bytes 1474592 | tf_op jit(solution)/shard_map/all_to_all | solution.py:87
  197.8 4.3 %all-to-all-start.3 = ((bf16[8,36,2560]{2,1,0:T(8,128)(2,1)}), bf16[8,36,2560]{2,1,0:T(8,128)(2,1)}, u32[]{:S(2)}, u32[]{:S(2)}) async-start(bf16[8,36,2560]{2,1,0:T(8,128)(2,1)} %fusion), calls=%async_computation.3 | async-start | bytes 3276800 | tf_op jit(solution)/shard_map/all_to_all | solution.py:91
  202.2 1.6 reshape.124
  203.7 2.5 gather_fusion
  206.3 4.2 %reshape.128 = f32[128,2,2560]{2,1,0:T(2,128)} reshape(bf16[256,2560]{1,0:T(8,128)(2,1)} %gather_fusion) | data formatting | bytes 3932160 | tf_op jit(solution)/shard_map/convert_element_type | solution.py:92
  210.5 0.4 fusion.10
  210.9 30.5 %all-to-all-done.3 = bf16[8,36,2560]{2,1,0:T(8,128)(2,1)} async-done(((bf16[8,36,2560]{2,1,0:T(8,128)(2,1)}), bf16[8,36,2560]{2,1,0:T(8,128)(2,1)}, u32[]{:S(2)}, u32[]{:S(2)}) %all-to-all-start.3) | async-done | bytes 1474592 | tf_op jit(solution)/shard_map/all_to_all | solution.py:91
  241.4 1.5 reshape.126
  242.9 2.5 gather_fusion.2
  245.5 4.1 %gather.18 = bf16[128,2,2560]{2,1,0:T(2,128)(2,1)} reshape(bf16[256,2560]{1,0:T(8,128)(2,1)} %gather_fusion.2) | data formatting | bytes 2621440 | tf_op jit(solution)/shard_map/gather | solution.py:97
  249.6 5.3 %reduce_sum.44 = bf16[128,2560]{1,0:T(8,128)(2,1)} reduce(bf16[128,2,2560]{2,1,0:T(2,128)(2,1)} %gather.18, bf16[]{:T(256)} %constant.31.clone.1), dimensions={1}, to_apply=%region_6.7 | reduce | flops 327680 | bytes 1966082 | tf_op jit(solution)/shard_map/reduce_sum | solution.py:98
  254.9 0.1 reshape.127
  255.0 0.6 copy.16
  255.7 4.5 %multiply_reduce_fusion = bf16[128,2560]{1,0:T(8,128)(2,1)} fusion(f32[128,2,2560]{2,1,0:T(2,128)S(1)} %copy-done.3, f32[128,2]{1,0:T(8,128)S(1)} %copy.11), kind=kLoop, calls=%fused_computation.22 | loop fusion | flops 983040 | bytes 3277824 | tf_op jit(solution)/shard_map/reduce_sum | solution.py:93
  (17 shorter events, 0.1 us)
Async XLA Ops:
  7.2 3.2 %copy-start = (bf16[128,2560]{1,0:T(8,128)(2,1)S(1)}, bf16[128,2560]{1,0:T(8,128)(2,1)}, u32[]{:S(2)}) copy-start(bf16[128,2560]{1,0:T(8,128)(2,1)} %param.7) | copy-start | bytes 1966084
  7.2 1.5 copy-start.5
  7.2 71.4 %all-gather.5.cloned.1.call-start = ((), (), s32[]{:S(2)}) async-start(), calls=%async_computation.4 | async-start | bytes 4915200 | tf_op jit(solution)/shard_map/all_gather | solution.py:77
  7.9 134.9 %all-gather.7.cloned.1.call-start = ((), (), s32[]{:S(2)}) async-start(), calls=%async_computation.5 | async-start | bytes 4915200 | tf_op jit(solution)/shard_map/all_gather | solution.py:78
  18.5 6.5 %copy-start.4 = (bf16[1,768,640]{2,1,0:T(8,128)(2,1)S(1)}, bf16[1,768,640]{2,1,0:T(8,128)(2,1)}, u32[]{:S(2)}) copy-start(bf16[1,768,640]{2,1,0:T(8,128)(2,1)} %param.12) | copy-start | bytes 2949124
  18.5 55.3 %all-to-all-start = ((bf16[8,36,2560]{2,1,0:T(8,128)(2,1)}), bf16[8,36,2560]{2,1,0:T(8,128)(2,1)}, u32[]{:S(2)}, u32[]{:S(2)}) async-start(bf16[8,36,2560]{2,1,0:T(8,128)(2,1)} %reshape.123), calls=%async_computation | async-start | bytes 3276800 | tf_op jit(solution)/shard_map/all_to_all | solution.py:82
  25.0 37.9 %collective-permute-start = (bf16[768,640]{1,0:T(8,128)(2,1)S(1)}, bf16[768,640]{1,0:T(8,128)(2,1)}, u32[]{:S(2)}, u32[]{:S(2)}) collective-permute-start(bf16[768,640]{1,0:T(8,128)(2,1)S(1)} %bitcast.33), channel_id=1, source_target_pairs={{0,8},{8,0},{16,24},{24,16},{1,9},{9,1},{17,25},{25,17},{2,10},{10... | collective-permute-start | bytes 2949128 | tf_op jit(solution)/shard_map/ppermute | solution.py:15
  26.6 41.2 %copy-start.6 = (f32[128,2]{0,1:T(2,128)S(1)}, f32[128,2]{0,1:T(2,128)}, u32[]{:S(2)}) copy-start(f32[128,2]{0,1:T(2,128)} %param.9) | copy-start | bytes 3076
  26.6 41.5 %copy-start.1 = (bf16[128,2560]{1,0:T(8,128)(2,1)S(1)}, bf16[128,2560]{1,0:T(8,128)(2,1)}, u32[]{:S(2)}) copy-start(bf16[128,2560]{1,0:T(8,128)(2,1)} %param.13) | copy-start | bytes 1966084
  66.3 80.5 %collective-permute-start.1 = (bf16[768,1280]{1,0:T(8,128)(2,1)}, bf16[768,1280]{1,0:T(8,128)(2,1)}, u32[]{:S(2)}, u32[]{:S(2)}) collective-permute-start(bf16[768,1280]{1,0:T(8,128)(2,1)} %maximum_select_fusion.1), channel_id=1, source_target_pairs={{0,16},{8,24},{16,0},{24,8},{1,17},{9,25},{17,1},{25,9},{2,18},{10... | collective-permute-start | bytes 5898248 | tf_op jit(solution)/shard_map/ppermute | solution.py:15
  73.8 80.3 %all-to-all-start.2 = ((bf16[8,36,2560]{2,1,0:T(8,128)(2,1)}), bf16[8,36,2560]{2,1,0:T(8,128)(2,1)}, u32[]{:S(2)}, u32[]{:S(2)}) async-start(bf16[8,36,2560]{2,1,0:T(8,128)(2,1)} %reshape.125), calls=%async_computation.2 | async-start | bytes 3276800 | tf_op jit(solution)/shard_map/all_to_all | solution.py:89
  146.9 0.9 copy-start.9
  154.1 43.8 %all-to-all-start.1 = ((bf16[8,36,2560]{2,1,0:T(8,128)(2,1)}), bf16[8,36,2560]{2,1,0:T(8,128)(2,1)}, u32[]{:S(2)}, u32[]{:S(2)}) async-start(bf16[8,36,2560]{2,1,0:T(8,128)(2,1)} %convolution_convert_fusion), calls=%async_computation.1 | async-start | bytes 3276800 | tf_op jit(solution)/shard_map/all_to_all | solution.py:87
  158.6 5.9 %copy-start.7 = (bf16[1,2560,768]{2,1,0:T(8,128)(2,1)S(1)}, bf16[1,2560,768]{2,1,0:T(8,128)(2,1)}, u32[]{:S(2)}) copy-start(bf16[1,2560,768]{2,1,0:T(8,128)(2,1)} %all-gather.5.cloned.1.call-done) | copy-start | bytes 11796484
  158.6 5.9 %copy-start.10 = (f32[8,36,768]{2,1,0:T(8,128)S(1)}, f32[8,36,768]{2,1,0:T(8,128)}, u32[]{:S(2)}) copy-start(f32[8,36,768]{2,1,0:T(8,128)} %copy-done.9) | copy-start | bytes 2654212
  164.5 2.1 copy-start.8
  197.8 43.5 %all-to-all-start.3 = ((bf16[8,36,2560]{2,1,0:T(8,128)(2,1)}), bf16[8,36,2560]{2,1,0:T(8,128)(2,1)}, u32[]{:S(2)}, u32[]{:S(2)}) async-start(bf16[8,36,2560]{2,1,0:T(8,128)(2,1)} %fusion), calls=%async_computation.3 | async-start | bytes 3276800 | tf_op jit(solution)/shard_map/all_to_all | solution.py:91
  206.3 4.2 %copy-start.2 = (bf16[256,2560]{1,0:T(8,128)(2,1)S(1)}, bf16[256,2560]{1,0:T(8,128)(2,1)}, u32[]{:S(2)}) copy-start(bf16[256,2560]{1,0:T(8,128)(2,1)} %gather_fusion) | copy-start | bytes 3932164
  245.5 10.2 %copy-start.3 = (f32[128,2,2560]{2,1,0:T(2,128)S(1)}, f32[128,2,2560]{2,1,0:T(2,128)}, u32[]{:S(2)}) copy-start(f32[128,2,2560]{2,1,0:T(2,128)} %reshape.128) | copy-start | bytes 7864324
Sparse Core Ops, SparseCore 0:
  9.9 66.0 all-gather.4
  77.8 64.9 all-gather.6
